TPU v7x, 32 devices: a whole 2x2x4 slice. The times are simulated.
32 devices in a mesh: dp: 4 (over x, core), expert: 8 (over z, y).
Axes of the slice: x: 2, y: 2, z: 4, core: 2. Of those that a mesh axis runs over, the one named last changes fastest.
Arguments:
- tokens: bfloat16 [256, 4096], P(('dp', 'expert')), may hold values from -6 to 6
- expert_ids: int32 [256, 8], P(('dp', 'expert')), may hold values from 0 to 31, all different within a row; in each aligned block of 8 rows (0 to 7, 8 to 15, ...) at most 4 rows name the same one
- gate_weights: float32 [256, 8], P(('dp', 'expert')), may hold values from 0.1 to 1
- gate_weight: bfloat16 [4096, 14336], P('dp', 'expert'), may hold values from -0.09375 to 0.09375
- up_weight: bfloat16 [4096, 14336], P('dp', 'expert'), may hold values from -0.09375 to 0.09375
- down_weight: bfloat16 [14336, 4096], P('expert', 'dp'), may hold values from -0.125 to 0.125
- expert_gain: float32 [4, 14336], P('dp', 'expert'), may hold values from 0.5 to 2
Outputs:
- mixed: bfloat16 [256, 4096], P(('dp', 'expert'))
Inputs may be any that keep to these rules, and one draw needn't show every extreme that they name: `expert_ids`: each row names 8 different experts. Among the 8 rows of one device no expert is named more than 4 times, a bound that some block reaches.
All inputs are finite; a program needn't handle non-finite values.
Results may differ from a plain program's by a relative error of at most 0.0055.
Values may be sent and summed in bfloat16 or wider, within the bound.
A program may use at most 128 MiB of HBM per device.

v0:
```python
import jax
import jax.numpy as jnp
from jax import lax
from jax.sharding import PartitionSpec as P

FF = 14336
EH = 1792


def slot_table(expert_ids, segments, capacity):
    tok_rows, top_count = expert_ids.shape
    flat_ids = expert_ids.reshape(-1)
    route_order = jnp.arange(flat_ids.shape[0], dtype=jnp.int32)
    earlier = (flat_ids[:, None] == flat_ids[None, :]) & (
        route_order[None, :] < route_order[:, None]
    )
    rank_in = jnp.sum(earlier.astype(jnp.int32), axis=1)
    copy_index = flat_ids // segments
    segment_index = flat_ids % segments
    group_index = copy_index * segments + segment_index
    return (group_index * capacity + rank_in).reshape(tok_rows, top_count)


def dispatch(tokens, position, slot_count):
    targets = jnp.arange(slot_count, dtype=jnp.int32)
    onehot = jnp.any(targets[:, None, None] == position[None, :, :], axis=2).astype(jnp.bfloat16)
    return jnp.dot(onehot, tokens, preferred_element_type=jnp.float32).astype(jnp.bfloat16)


def expert_block(routed, gate_weight, up_weight, down_weight, expert_gain):

    def add_rows(piece):
        return jnp.dot(routed, piece, preferred_element_type=jnp.float32)

    gate_sum = add_rows(lax.all_gather(gate_weight, "dp", axis=0, tiled=True))
    up_sum = add_rows(lax.all_gather(up_weight, "dp", axis=0, tiled=True))
    hidden = (jax.nn.silu(gate_sum) * up_sum * expert_gain).astype(jnp.bfloat16)
    partial_value = jnp.dot(
        hidden,
        lax.all_gather(down_weight, "dp", axis=1, tiled=True),
        preferred_element_type=jnp.float32,
    )
    return partial_value.astype(jnp.bfloat16)


def body(tokens, expert_ids, gate_weights, gate_weight, up_weight, down_weight, expert_gain):
    copies = lax.axis_size("dp")
    owners = lax.axis_size("expert")
    segments = FF // EH
    quarters = owners // segments
    tok_rows, top_count = expert_ids.shape
    model_width = tokens.shape[1]
    experts = copies * segments
    capacity = max(2, (2 * tok_rows * top_count + experts - 1) // experts)
    slot_count = experts * capacity
    position = slot_table(expert_ids, segments, capacity)
    buffer = dispatch(tokens, position, slot_count)
    sectioned = buffer.reshape(copies, segments, capacity, model_width)
    arrived = lax.all_to_all(sectioned, "dp", split_axis=0, concat_axis=2, tiled=True)
    spread = jnp.broadcast_to(
        arrived.reshape(segments, 1, copies * capacity, model_width),
        (segments, quarters, copies * capacity, model_width),
    )
    spread = spread.reshape(owners, copies * capacity, model_width)
    rows_in = lax.all_to_all(spread, "expert", split_axis=0, concat_axis=1, tiled=True)
    partial_value = expert_block(
        rows_in.reshape(-1, model_width), gate_weight, up_weight, down_weight, expert_gain
    )
    returned = lax.all_to_all(
        partial_value.reshape(1, owners * copies * capacity, model_width),
        "expert",
        split_axis=1,
        concat_axis=0,
        tiled=True,
    )
    summed = jnp.sum(
        returned.reshape(segments, quarters, copies * capacity, model_width).astype(jnp.float32),
        axis=1,
    )
    summed = summed.astype(jnp.bfloat16)
    at_home = lax.all_to_all(
        summed.reshape(1, segments, copies * capacity, model_width),
        "dp",
        split_axis=2,
        concat_axis=0,
        tiled=True,
    )
    results = at_home.reshape(slot_count, model_width)
    picked = jnp.take(results, position.reshape(-1), axis=0).reshape(
        tok_rows, top_count, model_width
    )
    mixed = jnp.sum(gate_weights[:, :, None] * picked.astype(jnp.float32), axis=1)
    return mixed.astype(jnp.bfloat16)


def solution(mesh):
    in_specs = (
        P(("dp", "expert"), None),
        P(("dp", "expert"), None),
        P(("dp", "expert"), None),
        P("dp", "expert"),
        P("dp", "expert"),
        P("expert", "dp"),
        P("dp", "expert"),
    )
    out_specs = P(("dp", "expert"), None)
    return jax.shard_map(body, mesh=mesh, in_specs=in_specs, out_specs=out_specs, check_vma=False)
```

profile of v0, /device:TPU:0, one launch (start us, length us, event | category | flops | bytes accessed | tf_op | source)
XLA Modules:
  0.0 390.4 jit_solution(17198120846166784655)
XLA Ops:
  6.5 0.7 all-gather.4.cloned.1.call-update
  8.7 0.8 reshape.204
  9.8 0.7 compare_and_fusion
  12.1 24.4 %all_to_all.51 = bf16[4,8,4,4096]{3,1,2,0:T(8,128)(2,1)S(1)} all-to-all(bf16[4,8,4,4096]{3,1,2,0:T(8,128)(2,1)S(1)} %copy.24), channel_id=1, replica_groups=mesh['dp'=4,'expert'=8] {'dp'}, dimensions={0} | all-to-all | bytes 2097152 | tf_op jit(solution)/shard_map/all_to_all | solution.py:59
  36.5 1.6 copy.25
  38.1 6.2 %all-to-all-start.1 = ((bf16[8,16,4096]{2,1,0:T(8,128)(2,1)}), bf16[8,16,4096]{2,1,0:T(8,128)(2,1)S(1)}, u32[]{:S(2)}, u32[]{:S(2)}) async-start(bf16[8,16,4096]{2,1,0:T(8,128)(2,1)} %copy.25), calls=%async_computation.1 | async-start | bytes 2097152 | tf_op jit(solution)/shard_map/all_to_all | solution.py:65
  44.3 25.3 %all-to-all-done.1 = bf16[8,16,4096]{2,1,0:T(8,128)(2,1)S(1)} async-done(((bf16[8,16,4096]{2,1,0:T(8,128)(2,1)}), bf16[8,16,4096]{2,1,0:T(8,128)(2,1)S(1)}, u32[]{:S(2)}, u32[]{:S(2)}) %all-to-all-start.1) | async-done | bytes 1048608 | tf_op jit(solution)/shard_map/all_to_all | solution.py:65
  69.6 41.7 %all-gather.4.cloned.1.call-done = bf16[4096,1792]{1,0:T(8,128)(2,1)} async-done(((bf16[1024,1792]{1,0:T(8,128)(2,1)}), bf16[4096,1792]{1,0:T(8,128)(2,1)}) %all-gather.4.cloned.1.call-update) | async-done | bytes 14680080 | tf_op jit(solution)/shard_map/all_gather | solution.py:35
  111.3 7.2 %fusion.19 = f32[128,1792]{1,0:T(8,128)S(1)} fusion(bf16[128,4096]{1,0:T(8,128)(2,1)S(1)} %bitcast.36, bf16[4096,1792]{1,0:T(8,128)(2,1)} %all-gather.4.cloned.1.call-done), kind=kOutput, calls=%fused_computation.45 | convolution fusion | flops 1879048192 | bytes 16646144 | tf_op jit(solution)/shard_map/dot_general | solution.py:33
  118.5 88.7 %all-gather.6.cloned.1.call-done = bf16[4096,1792]{1,0:T(8,128)(2,1)} async-done(((bf16[1024,1792]{1,0:T(8,128)(2,1)}), bf16[4096,1792]{1,0:T(8,128)(2,1)}) %all-gather.6.cloned.1.call-update) | async-done | bytes 14680080 | tf_op jit(solution)/shard_map/all_gather | solution.py:36
  207.2 95.6 %all-gather.8.cloned.1.call-done = bf16[1792,4096]{1,0:T(8,128)(2,1)} async-done(((bf16[1792,1024]{1,0:T(8,128)(2,1)}), bf16[1792,4096]{1,0:T(8,128)(2,1)}) %all-gather.8.cloned.1.call-update) | async-done | bytes 14680080 | tf_op jit(solution)/shard_map/all_gather | solution.py:40
  302.8 13.8 %fusion = bf16[1,128,4096]{2,1,0:T(8,128)(2,1)S(1)} fusion(bf16[1792,4096]{1,0:T(8,128)(2,1)} %all-gather.8.cloned.1.call-done, bf16[128,4096]{1,0:T(8,128)(2,1)S(1)} %bitcast.37, bf16[4096,1792]{1,0:T(8,128)(2,1)} %all-gather.6.cloned.1.call-done, f32[128,1792]{1,0:T(8,128)S(1)} %fusion.19, f32[1792]{0:T(1024)S(1)} %reduce), kind=kOutput, calls=%fused_computation.3 | convolution fusion | flops 3760226304 | bytes 32381952 | tf_op jit(solution)/shard_map/dot_general | solution.py:38
  316.7 2.4 copy.33
  319.6 7.2 %reduce.1 = bf16[128,4096]{1,0:T(8,128)(2,1)S(1)} reduce(bf16[128,1,4096]{2,1,0:T(2,128)(2,1)S(1)} %bitcast.39, bf16[]{:T(256)} %broadcast.207), dimensions={1}, to_apply=%bitcast.35.reduce_sub_computation | reduce | bytes 2097154
  326.8 0.8 reshape.219
  327.6 31.5 %all_to_all.52 = bf16[8,2,32768]{2,1,0:T(2,128)(2,1)S(1)} all-to-all(bf16[8,2,32768]{2,1,0:T(2,128)(2,1)S(1)} %reshape.219), channel_id=1, replica_groups=mesh['dp'=4,'expert'=8] {'expert'}, dimensions={0} | all-to-all | bytes 2097152 | tf_op jit(solution)/shard_map/all_to_all | solution.py:69
  359.1 1.0 reshape.220
  360.1 1.1 copy.29
  361.3 1.5 copy.27
  362.8 3.5 all-to-all-start.3
  366.5 14.3 %all-to-all-done.3 = bf16[1,8,16,4096]{3,1,0,2:T(8,128)(2,1)S(1)} async-done(((bf16[1,8,16,4096]{3,1,0,2:T(8,128)(2,1)}), bf16[1,8,16,4096]{3,1,0,2:T(8,128)(2,1)S(1)}, u32[]{:S(2)}, u32[]{:S(2)}) %all-to-all-start.3) | async-done | bytes 1048608 | tf_op jit(solution)/shard_map/all_to_all | solution.py:81
  380.8 0.8 copy.32
  381.9 0.9 gather_fusion
  382.8 1.1 multiply_reduce_fusion
  (27 shorter events, 4.2 us)
Async XLA Ops:
  6.5 4.1 %copy-start = (bf16[8,4096]{1,0:T(8,128)(2,1)S(1)}, bf16[8,4096]{1,0:T(8,128)(2,1)}, u32[]{:S(2)}) copy-start(bf16[8,4096]{1,0:T(8,128)(2,1)} %param.7) | copy-start | bytes 196612
  6.5 37.7 %copy-start.3 = (f32[1,1792]{1,0:T(1,128)S(1)}, f32[1,1792]{1,0:T(1,128)}, u32[]{:S(2)}) copy-start(f32[1,1792]{1,0:T(1,128)} %param.13) | copy-start | bytes 21508
  6.5 104.8 %all-gather.4.cloned.1.call-start = ((), (), s32[]{:S(2)}) async-start(), calls=%async_computation.4 | async-start | bytes 18350080 | tf_op jit(solution)/shard_map/all_gather | solution.py:35
  7.3 200.0 %all-gather.6.cloned.1.call-start = ((), (), s32[]{:S(2)}) async-start(), calls=%async_computation.5 | async-start | bytes 18350080 | tf_op jit(solution)/shard_map/all_gather | solution.py:36
  8.0 294.8 %all-gather.8.cloned.1.call-start = ((), (), s32[]{:S(2)}) async-start(), calls=%async_computation.6 | async-start | bytes 18350080 | tf_op jit(solution)/shard_map/all_gather | solution.py:40
  38.1 31.5 %all-to-all-start.1 = ((bf16[8,16,4096]{2,1,0:T(8,128)(2,1)}), bf16[8,16,4096]{2,1,0:T(8,128)(2,1)S(1)}, u32[]{:S(2)}, u32[]{:S(2)}) async-start(bf16[8,16,4096]{2,1,0:T(8,128)(2,1)} %copy.25), calls=%async_computation.1 | async-start | bytes 2097152 | tf_op jit(solution)/shard_map/all_to_all | solution.py:65
  302.8 81.0 %copy-start.1 = (bf16[8,4096]{1,0:T(8,128)(2,1)S(1)}, bf16[8,4096]{1,0:T(8,128)(2,1)}, u32[]{:S(2)}) copy-start(bf16[8,4096]{1,0:T(8,128)(2,1)} %param.7) | copy-start | bytes 196612
  316.6 49.7 %copy-start.2 = (s32[8,8]{1,0:T(8,128)S(1)}, s32[8,8]{1,0:T(8,128)}, u32[]{:S(2)}) copy-start(s32[8,8]{1,0:T(8,128)} %param.8) | copy-start | bytes 772
  316.7 66.1 %copy-start.4 = (f32[8,8]{1,0:T(8,128)S(1)}, f32[8,8]{1,0:T(8,128)}, u32[]{:S(2)}) copy-start(f32[8,8]{1,0:T(8,128)} %param.9) | copy-start | bytes 772
  362.8 18.0 %all-to-all-start.3 = ((bf16[1,8,16,4096]{3,1,0,2:T(8,128)(2,1)}), bf16[1,8,16,4096]{3,1,0,2:T(8,128)(2,1)S(1)}, u32[]{:S(2)}, u32[]{:S(2)}) async-start(bf16[1,8,16,4096]{3,1,0,2:T(8,128)(2,1)} %copy.27), calls=%async_computation.3 | async-start | bytes 2097152 | tf_op jit(solution)/shard_map/all_to_all | solution.py:81
Sparse Core Ops, SparseCore 0:
  8.9 102.3 all-gather.3
  112.8 94.3 all-gather.5
  208.8 94.0 all-gather.7
where the time goes:
time: 391 us; the launch traced here: 390 us
  waiting for transfers between devices  268 us (69%)
  blocking collectives  55.9 us (14%)
  matrix products  21.5 us (5%)
  between operations  13.3 us (3%)
  local copies, waits for them, and re-layouts  12.9 us (3%)
  starting transfers between devices  9.76 us (2%)
  other arithmetic  9.34 us (2%)
    all_gather x1, waiting for transfers between devices, expert_block(): lax.all_gather(down_weight, 'dp', axis=1, tiled=True)  95.6 us
    all_gather x1, waiting for transfers between devices, expert_block(): up_sum = add_rows(lax.all_gather(up_weight, 'dp', axis=0, tiled=True))  88.7 us
    all_gather x1, waiting for transfers between devices, expert_block(): gate_sum = add_rows(lax.all_gather(gate_weight, 'dp', axis=0, tiled=True))  41.7 us
    all_to_all x1, blocking collectives, body(): lax.all_to_all(partial_value.reshape(1, owners * copies * capacity, model...  31.5 us
    all_to_all x1, waiting for transfers between devices, body(): lax.all_to_all(spread, 'expert', split_axis=0, concat_axis=1, tiled=True)  25.3 us
    all_to_all x1, blocking collectives, body(): lax.all_to_all(sectioned, 'dp', split_axis=0, concat_axis=2, tiled=True)  24.4 us
    all_to_all x1, waiting for transfers between devices, body(): lax.all_to_all(summed.reshape(1, segments, copies * capacity, model_width...  14.3 us
    dot_general x1, matrix products, expert_block(): jnp.dot(hidden, lax.all_gather(down_weight, 'dp', axis=1, tiled=True), pr...  13.8 us
  transfers between devices with their start and end apart: 5, of which 5 were waited for; matrix products, arithmetic and copies ran while one was open for 3% of the time, Pallas kernels for 0%

commit v1 on v0

--- a/solution.py
+++ b/solution.py
@@ -5,6 +5,17 @@
 
 FF = 14336
 EH = 1792
+
+
+def in_blocks(x, dim, size):
+    before, after = (x.shape[:dim], x.shape[dim + 1 :])
+    return jnp.moveaxis(x.reshape(*before, size, -1, *after), dim, 0)
+
+
+def in_order(blocks, dim):
+    blocks = jnp.moveaxis(blocks, 0, dim)
+    dims = blocks.shape
+    return blocks.reshape(*dims[:dim], dims[dim] * dims[dim + 1], *dims[dim + 2 :])
 
 
 def slot_table(expert_ids, segments, capacity):
@@ -78,13 +89,15 @@
         axis=1,
     )
     summed = summed.astype(jnp.bfloat16)
-    at_home = lax.all_to_all(
-        summed.reshape(1, segments, copies * capacity, model_width),
-        "dp",
-        split_axis=2,
-        concat_axis=0,
-        tiled=True,
-    )
+    value = summed.reshape(1, segments, copies * capacity, model_width)
+    peers, here = (lax.axis_size("dp"), lax.axis_index("dp"))
+    blocks = in_blocks(value, 2, peers)
+    gathered = [blocks[here]]
+    for turn in range(1, peers):
+        sent = blocks[here ^ turn]
+        gathered.append(lax.ppermute(sent, "dp", [(i, i ^ turn) for i in range(peers)]))
+    blocks = jnp.stack(gathered)[here ^ jnp.arange(peers)]
+    at_home = in_order(blocks, 0)
     results = at_home.reshape(slot_count, model_width)
     picked = jnp.take(results, position.reshape(-1), axis=0).reshape(
         tok_rows, top_count, model_width

time: 391 us -> 393 us (level)
  blocking collectives: 55.9 us -> 24.4 us
  waiting for transfers between devices: 268 us -> 290 us
  local copies, waits for them, and re-layouts: 12.9 us -> 18.8 us
  starting transfers between devices: 9.76 us -> 14 us
    all_to_all x1 -> x0, blocking collectives: 31.5 us -> none  [body(): lax.all_to_all(partial_value.reshape(1, owners * copies * capacity, model...]
    all_to_all x1, waiting for transfers between devices: 14.3 us -> 26.1 us  [body(): lax.all_to_all(partial_value.reshape(1, owners * copies * capacity, model...]
    ppermute x0 -> x3, waiting for transfers between devices: none -> 10.8 us  [body(): lax.ppermute(sent, 'dp', [(i, i ^ turn) for i in range(peers)])]
    all_to_all x1, local copies, waits for them, and re-layouts: 1.55 us -> 6.21 us  [body(): lax.all_to_all(partial_value.reshape(1, owners * copies * capacity, model...]
  transfers between devices with their start and end apart: 5 -> 8, of which waited for: 5 -> 7; matrix products, arithmetic and copies ran while one was open for 3% -> 3% of each run, Pallas kernels for 0% -> 0%
where the time goes in v1:
time: 393 us; the launch traced here: 392 us
  waiting for transfers between devices  290 us (74%)
  blocking collectives  24.4 us (6%)
  matrix products  21.5 us (5%)
  local copies, waits for them, and re-layouts  18.8 us (5%)
  starting transfers between devices  14 us (4%)
  between operations  13.3 us (3%)
  other arithmetic  10.3 us (3%)
    all_gather x1, waiting for transfers between devices, expert_block(): lax.all_gather(down_weight, 'dp', axis=1, tiled=True)  95.6 us
    all_gather x1, waiting for transfers between devices, expert_block(): up_sum = add_rows(lax.all_gather(up_weight, 'dp', axis=0, tiled=True))  88.7 us
    all_gather x1, waiting for transfers between devices, expert_block(): gate_sum = add_rows(lax.all_gather(gate_weight, 'dp', axis=0, tiled=True))  41.7 us
    all_to_all x1, waiting for transfers between devices, body(): lax.all_to_all(partial_value.reshape(1, owners * copies * capacity, model...  26.1 us
    all_to_all x1, waiting for transfers between devices, body(): lax.all_to_all(spread, 'expert', split_axis=0, concat_axis=1, tiled=True)  25.3 us
    all_to_all x1, blocking collectives, body(): lax.all_to_all(sectioned, 'dp', split_axis=0, concat_axis=2, tiled=True)  24.4 us
    dot_general x1, matrix products, expert_block(): jnp.dot(hidden, lax.all_gather(down_weight, 'dp', axis=1, tiled=True), pr...  13.8 us
    ppermute x3, waiting for transfers between devices, body(): lax.ppermute(sent, 'dp', [(i, i ^ turn) for i in range(peers)])  10.8 us
  transfers between devices with their start and end apart: 8, of which 7 were waited for; matrix products, arithmetic and copies ran while one was open for 3% of the time, Pallas kernels for 0%

profile of v1, /device:TPU:0, one launch (start us, length us, event | category | flops | bytes accessed | tf_op | source)
XLA Modules:
  0.0 392.5 jit_solution(5722571389339369443)
XLA Ops:
  8.7 0.8 reshape.226
  12.1 24.4 %all_to_all.33 = bf16[4,8,4,4096]{3,1,2,0:T(8,128)(2,1)S(1)} all-to-all(bf16[4,8,4,4096]{3,1,2,0:T(8,128)(2,1)S(1)} %copy.17), channel_id=1, replica_groups=mesh['dp'=4,'expert'=8] {'dp'}, dimensions={0} | all-to-all | bytes 2097152 | tf_op jit(solution)/shard_map/all_to_all | solution.py:70
  36.5 1.6 copy.18
  38.1 6.2 %all-to-all-start.1 = ((bf16[8,16,4096]{2,1,0:T(8,128)(2,1)}), bf16[8,16,4096]{2,1,0:T(8,128)(2,1)S(1)}, u32[]{:S(2)}, u32[]{:S(2)}) async-start(bf16[8,16,4096]{2,1,0:T(8,128)(2,1)} %copy.18), calls=%async_computation.1 | async-start | bytes 2097152 | tf_op jit(solution)/shard_map/all_to_all | solution.py:76
  44.3 25.3 %all-to-all-done.1 = bf16[8,16,4096]{2,1,0:T(8,128)(2,1)S(1)} async-done(((bf16[8,16,4096]{2,1,0:T(8,128)(2,1)}), bf16[8,16,4096]{2,1,0:T(8,128)(2,1)S(1)}, u32[]{:S(2)}, u32[]{:S(2)}) %all-to-all-start.1) | async-done | bytes 1048608 | tf_op jit(solution)/shard_map/all_to_all | solution.py:76
  69.6 41.7 %all-gather.4.cloned.1.call-done = bf16[4096,1792]{1,0:T(8,128)(2,1)} async-done(((bf16[1024,1792]{1,0:T(8,128)(2,1)}), bf16[4096,1792]{1,0:T(8,128)(2,1)}) %all-gather.4.cloned.1.call-update) | async-done | bytes 14680080 | tf_op jit(solution)/shard_map/all_gather | solution.py:46
  111.3 7.2 %fusion.20 = f32[128,1792]{1,0:T(8,128)S(1)} fusion(bf16[128,4096]{1,0:T(8,128)(2,1)S(1)} %bitcast.45, bf16[4096,1792]{1,0:T(8,128)(2,1)} %all-gather.4.cloned.1.call-done), kind=kOutput, calls=%fused_computation.54 | convolution fusion | flops 1879048192 | bytes 16646144 | tf_op jit(solution)/shard_map/dot_general | solution.py:44
  118.6 88.7 %all-gather.6.cloned.1.call-done = bf16[4096,1792]{1,0:T(8,128)(2,1)} async-done(((bf16[1024,1792]{1,0:T(8,128)(2,1)}), bf16[4096,1792]{1,0:T(8,128)(2,1)}) %all-gather.6.cloned.1.call-update) | async-done | bytes 14680080 | tf_op jit(solution)/shard_map/all_gather | solution.py:47
  207.2 95.6 %all-gather.8.cloned.1.call-done = bf16[1792,4096]{1,0:T(8,128)(2,1)} async-done(((bf16[1792,1024]{1,0:T(8,128)(2,1)}), bf16[1792,4096]{1,0:T(8,128)(2,1)}) %all-gather.8.cloned.1.call-update) | async-done | bytes 14680080 | tf_op jit(solution)/shard_map/all_gather | solution.py:51
  302.8 13.8 %fusion = bf16[1,128,4096]{2,1,0:T(8,128)(2,1)S(1)} fusion(bf16[1792,4096]{1,0:T(8,128)(2,1)} %all-gather.8.cloned.1.call-done, bf16[128,4096]{1,0:T(8,128)(2,1)S(1)} %bitcast.46, bf16[4096,1792]{1,0:T(8,128)(2,1)} %all-gather.6.cloned.1.call-done, f32[128,1792]{1,0:T(8,128)S(1)} %fusion.20, f32[1792]{0:T(1024)S(1)} %reduce), kind=kOutput, calls=%fused_computation.4 | convolution fusion | flops 3760226304 | bytes 32381952 | tf_op jit(solution)/shard_map/dot_general | solution.py:49
  316.6 2.4 copy.22
  319.5 7.2 %reduce.3 = bf16[128,4096]{1,0:T(8,128)(2,1)S(1)} reduce(bf16[128,1,4096]{2,1,0:T(2,128)(2,1)S(1)} %bitcast.47, bf16[]{:T(256)} %broadcast.252), dimensions={1}, to_apply=%bitcast.44.reduce_sub_computation | reduce | bytes 2097154
  326.8 1.6 reshape.253
  328.4 5.5 %all-to-all-start.2 = ((bf16[8,2,32768]{2,1,0:T(2,128)(2,1)}), bf16[8,2,32768]{2,1,0:T(2,128)(2,1)S(1)}, u32[]{:S(2)}, u32[]{:S(2)}) async-start(bf16[8,2,32768]{2,1,0:T(2,128)(2,1)} %reshape.253), calls=%async_computation.2 | async-start | bytes 2097152 | tf_op jit(solution)/shard_map/all_to_all | solution.py:80
  334.0 26.1 %all-to-all-done.2 = bf16[8,2,32768]{2,1,0:T(2,128)(2,1)S(1)} async-done(((bf16[8,2,32768]{2,1,0:T(2,128)(2,1)}), bf16[8,2,32768]{2,1,0:T(2,128)(2,1)S(1)}, u32[]{:S(2)}, u32[]{:S(2)}) %all-to-all-start.2) | async-done | bytes 1048608 | tf_op jit(solution)/shard_map/all_to_all | solution.py:80
  360.1 1.0 reshape.254
  361.1 6.2 %bitcast_reduce_fusion = bf16[128,4096]{1,0:T(8,128)(2,1)S(1)} fusion(bf16[128,1,4096]{2,1,0:T(2,128)(2,1)S(1)} %reshape.254), kind=kLoop, calls=%fused_computation.52 | loop fusion | bytes 2097152 | tf_op jit(solution)/shard_map/all_to_all | solution.py:80
  369.1 1.5 collective-permute-start.1
  370.5 6.4 %collective-permute-done.2 = bf16[1,8,4,4096]{3,2,1,0:T(4,128)(2,1)S(1)} collective-permute-done((bf16[1,8,4,4096]{3,2,1,0:T(4,128)(2,1)S(1)}, bf16[1,8,4,4096]{3,2,1,0:T(4,128)(2,1)S(1)}, u32[]{:S(2)}, u32[]{:S(2)}) %collective-permute-start.2) | collective-permute-done | bytes 262176 | tf_op jit(solution)/shard_map/ppermute | solution.py:98
  376.9 4.4 %collective-permute-done.1 = bf16[1,8,4,4096]{3,2,1,0:T(4,128)(2,1)S(1)} collective-permute-done((bf16[1,8,4,4096]{3,2,1,0:T(4,128)(2,1)S(1)}, bf16[1,8,4,4096]{3,2,1,0:T(4,128)(2,1)S(1)}, u32[]{:S(2)}, u32[]{:S(2)}) %collective-permute-start.1) | collective-permute-done | bytes 262176 | tf_op jit(solution)/shard_map/ppermute | solution.py:98
  381.3 1.0 maximum_bitcast_fusion
  382.3 1.4 gather_fusion
  384.0 0.9 gather_fusion.1
  384.9 1.1 multiply_reduce_fusion
  (36 shorter events, 7.4 us)
Async XLA Ops:
  6.5 4.1 %copy-start = (bf16[8,4096]{1,0:T(8,128)(2,1)S(1)}, bf16[8,4096]{1,0:T(8,128)(2,1)}, u32[]{:S(2)}) copy-start(bf16[8,4096]{1,0:T(8,128)(2,1)} %param.7) | copy-start | bytes 196612
  6.5 37.7 %copy-start.3 = (f32[1,1792]{1,0:T(1,128)S(1)}, f32[1,1792]{1,0:T(1,128)}, u32[]{:S(2)}) copy-start(f32[1,1792]{1,0:T(1,128)} %param.13) | copy-start | bytes 21508
  6.5 104.8 %all-gather.4.cloned.1.call-start = ((), (), s32[]{:S(2)}) async-start(), calls=%async_computation.3 | async-start | bytes 18350080 | tf_op jit(solution)/shard_map/all_gather | solution.py:46
  7.3 200.0 %all-gather.6.cloned.1.call-start = ((), (), s32[]{:S(2)}) async-start(), calls=%async_computation.4 | async-start | bytes 18350080 | tf_op jit(solution)/shard_map/all_gather | solution.py:47
  8.0 294.8 %all-gather.8.cloned.1.call-start = ((), (), s32[]{:S(2)}) async-start(), calls=%async_computation.5 | async-start | bytes 18350080 | tf_op jit(solution)/shard_map/all_gather | solution.py:51
  38.1 31.5 %all-to-all-start.1 = ((bf16[8,16,4096]{2,1,0:T(8,128)(2,1)}), bf16[8,16,4096]{2,1,0:T(8,128)(2,1)S(1)}, u32[]{:S(2)}, u32[]{:S(2)}) async-start(bf16[8,16,4096]{2,1,0:T(8,128)(2,1)} %copy.18), calls=%async_computation.1 | async-start | bytes 2097152 | tf_op jit(solution)/shard_map/all_to_all | solution.py:76
  118.5 215.3 %copy-start.2 = (s32[8,8]{1,0:T(8,128)S(1)}, s32[8,8]{1,0:T(8,128)}, u32[]{:S(2)}) copy-start(s32[8,8]{1,0:T(8,128)} %param.8) | copy-start | bytes 772
  319.0 65.9 %copy-start.4 = (f32[8,8]{1,0:T(8,128)S(1)}, f32[8,8]{1,0:T(8,128)}, u32[]{:S(2)}) copy-start(f32[8,8]{1,0:T(8,128)} %param.9) | copy-start | bytes 772
  319.0 67.0 %copy-start.1 = (bf16[8,4096]{1,0:T(8,128)(2,1)S(1)}, bf16[8,4096]{1,0:T(8,128)(2,1)}, u32[]{:S(2)}) copy-start(bf16[8,4096]{1,0:T(8,128)(2,1)} %param.7) | copy-start | bytes 196612
  328.4 31.7 %all-to-all-start.2 = ((bf16[8,2,32768]{2,1,0:T(2,128)(2,1)}), bf16[8,2,32768]{2,1,0:T(2,128)(2,1)S(1)}, u32[]{:S(2)}, u32[]{:S(2)}) async-start(bf16[8,2,32768]{2,1,0:T(2,128)(2,1)} %reshape.253), calls=%async_computation.2 | async-start | bytes 2097152 | tf_op jit(solution)/shard_map/all_to_all | solution.py:80
  368.3 8.6 %collective-permute-start.2 = (bf16[1,8,4,4096]{3,2,1,0:T(4,128)(2,1)S(1)}, bf16[1,8,4,4096]{3,2,1,0:T(4,128)(2,1)S(1)}, u32[]{:S(2)}, u32[]{:S(2)}) collective-permute-start(bf16[1,8,4,4096]{3,2,1,0:T(4,128)(2,1)S(1)} %get-tuple-element.8), channel_id=1, source_target_pairs={{0,24},{8,16},{16,8},{24,0},{1,25},{9,17},{17,9},{25,1},{2,26},{10... | collective-permute-start | bytes 786440 | tf_op jit(solution)/shard_map/ppermute | solution.py:98
  368.4 8.5 %collective-permute-start = (bf16[1,8,4,4096]{3,2,1,0:T(4,128)(2,1)S(1)}, bf16[1,8,4,4096]{3,2,1,0:T(4,128)(2,1)S(1)}, u32[]{:S(2)}, u32[]{:S(2)}) collective-permute-start(bf16[1,8,4,4096]{3,2,1,0:T(4,128)(2,1)S(1)} %get-tuple-element.10), channel_id=1, source_target_pairs={{0,8},{8,0},{16,24},{24,16},{1,9},{9,1},{17,25},{25,17},{2,10},{10... | collective-permute-start | bytes 786440 | tf_op jit(solution)/shard_map/ppermute | solution.py:98
  369.1 12.3 %collective-permute-start.1 = (bf16[1,8,4,4096]{3,2,1,0:T(4,128)(2,1)S(1)}, bf16[1,8,4,4096]{3,2,1,0:T(4,128)(2,1)S(1)}, u32[]{:S(2)}, u32[]{:S(2)}) collective-permute-start(bf16[1,8,4,4096]{3,2,1,0:T(4,128)(2,1)S(1)} %get-tuple-element.9), channel_id=1, source_target_pairs={{0,16},{8,24},{16,0},{24,8},{1,17},{9,25},{17,1},{25,9},{2,18},{10... | collective-permute-start | bytes 786440 | tf_op jit(solution)/shard_map/ppermute | solution.py:98
Sparse Core Ops, SparseCore 0:
  8.9 102.3 all-gather.3
  112.8 94.3 all-gather.5
  208.8 94.0 all-gather.7
